TPU v7x, 1024 devices: a whole 4x8x16 slice. The times are simulated.
1024 devices in a mesh: dp: 128 (over z_hi, x, y, core), expert: 8 (over z_lo).
Axes of the slice: x: 4, y: 8, z: 16 (z_hi: 2, z_lo: 8; z = z_hi * 8 + z_lo), core: 2. Of those that a mesh axis runs over, the one named last changes fastest.
Arguments:
- picture_vectors: bfloat16 [393216, 1024], P(('dp', 'expert')), may hold values from -1 to 1
- caption_vectors: bfloat16 [65536, 1024], P(('dp', 'expert')), may hold values from -1 to 1
- projector_inputs: bfloat16 [393216, 640], P(('dp', 'expert')), may hold values from -0.017944336 to 0.017944336
- assigned_specialist: int32 [393216, 1], P(('dp', 'expert')), may hold values from 0 to 7; in each aligned block of 384 rows (0 to 383, 384 to 767, ...) at most 60 rows name the same one
- score_multiplier: float32 [1], replicated, may hold values from 1 to 4
- score_shift: float32 [1], replicated, may hold values from -2 to 0
Outputs:
- image_loss: float32 [393216], P(('dp', 'expert'))
- text_grad: float32 [65536, 1024], P(('dp', 'expert'))
- expert_grad: float32 [8, 1024, 640], P('expert', 'dp')
Inputs may be any that keep to these rules, and one draw needn't show every extreme that they name: `assigned_specialist`: among the images of one device at most 60 name any one expert, and in every draw some expert is named by exactly 60 of them on some device; every expert is named somewhere.
All inputs are finite; a program needn't handle non-finite values.
Results may differ from a plain program's by a relative error of at most 0.0037.
Values may be sent and summed in bfloat16 or wider, within the bound.
A program may use at most 32 MiB of HBM per device.

v0:
```python
import jax
import jax.numpy as jnp
from jax import lax
from jax.sharding import PartitionSpec as P

STEPS = 4


def from_behind(value, axis, steps):
    count = lax.axis_size(axis)
    pairs = [(source, (source + steps) % count) for source in range(count)]
    return lax.ppermute(value, axis, pairs)


def couple_contributions(picture_batch, caption_batch, score_scaling, neighbour_shift, match_signs):
    pair_scores = (
        score_scaling
        * lax.dot_general(
            picture_batch,
            caption_batch,
            (((1,), (1,)), ((), ())),
            preferred_element_type=jnp.float32,
        )
        + neighbour_shift
    )
    couple_penalty = jnp.sum(jax.nn.softplus(-match_signs * pair_scores), axis=1)
    specialist_projector = (
        -score_scaling * match_signs * jax.nn.sigmoid(-match_signs * pair_scores)
    ).astype(jnp.bfloat16)
    return (couple_penalty, specialist_projector)


def contract_rows(specialist_projector, picture_batch):
    return lax.dot_general(
        specialist_projector,
        picture_batch,
        (((0,), (0,)), ((), ())),
        preferred_element_type=jnp.float32,
    )


def on_device(
    picture_vectors,
    caption_vectors,
    projector_inputs,
    assigned_specialist,
    score_multiplier,
    score_shift,
):
    score_scaling = score_multiplier[0]
    neighbour_shift = score_shift[0]
    img_rows = picture_vectors.shape[0]
    txt_rows = caption_vectors.shape[0]
    matches = (jnp.arange(img_rows) // 2)[:, None] == jnp.arange(txt_rows)[None, :]
    diagonal_labels = jnp.where(matches, 1.0, -1.0).astype(jnp.float32)
    other_labels = jnp.full((img_rows, txt_rows), -1.0, jnp.float32)
    caption_batch = caption_vectors
    total_loss = jnp.zeros((img_rows,), jnp.float32)
    image_grad = jnp.zeros((img_rows, picture_vectors.shape[1]), jnp.float32)
    carried = None
    text_grad = None
    for step in range(STEPS):
        if step > 0:
            caption_batch = from_behind(caption_batch, "dp", 1)
        match_signs = diagonal_labels if step == 0 else other_labels
        couple_penalty, specialist_projector = couple_contributions(
            picture_vectors, caption_batch, score_scaling, neighbour_shift, match_signs
        )
        total_loss = total_loss + couple_penalty
        image_grad = image_grad + jnp.dot(
            specialist_projector, caption_batch, preferred_element_type=jnp.float32
        )
        partial_value = contract_rows(specialist_projector, picture_vectors)
        if step == 0:
            carried = partial_value
        else:
            carried = from_behind(carried, "dp", 1) + partial_value
    text_grad = from_behind(carried, "dp", 1 - STEPS)
    grads = image_grad.astype(jnp.bfloat16)
    owners = lax.axis_size("expert")
    capacity = 5 * img_rows // (4 * owners)
    target = assigned_specialist[:, 0]
    onehot = (target[:, None] == jnp.arange(owners, dtype=jnp.int32)[None, :]).astype(jnp.int32)
    slot_index = jnp.sum((jnp.cumsum(onehot, axis=0) - 1) * onehot, axis=1)
    destination = target * capacity + slot_index
    feat_width = projector_inputs.shape[1]
    grad_width = grads.shape[1]
    feat_buffer = (
        jnp.zeros((owners * capacity, feat_width), jnp.bfloat16)
        .at[destination]
        .set(projector_inputs)
    )
    grad_buffer = (
        jnp.zeros((owners * capacity, grad_width), jnp.bfloat16).at[destination].set(grads)
    )
    feat_recv, grad_recv = (
        lax.all_to_all(
            feat_buffer.reshape(owners, capacity, feat_width),
            "expert",
            split_axis=0,
            concat_axis=0,
            tiled=True,
        ),
        lax.all_to_all(
            grad_buffer.reshape(owners, capacity, grad_width),
            "expert",
            split_axis=0,
            concat_axis=0,
            tiled=True,
        ),
    )
    feat_recv = feat_recv.reshape(owners * capacity, feat_width)
    grad_recv = grad_recv.reshape(owners * capacity, grad_width)
    grad_rows = lax.psum_scatter(
        lax.dot_general(
            grad_recv, feat_recv, (((0,), (0,)), ((), ())), preferred_element_type=jnp.float32
        ),
        "dp",
        scatter_dimension=0,
        tiled=True,
    )
    return (total_loss, text_grad, grad_rows[None])


def solution(mesh):
    return jax.shard_map(
        on_device,
        mesh=mesh,
        in_specs=(
            P(("dp", "expert"), None),
            P(("dp", "expert"), None),
            P(("dp", "expert"), None),
            P(("dp", "expert"), None),
            P(),
            P(),
        ),
        out_specs=(P(("dp", "expert")), P(("dp", "expert"), None), P("expert", "dp", None)),
        check_vma=False,
    )
```

profile of v0, /device:TPU:64, one launch (start us, length us, event | category | flops | bytes accessed | tf_op | source)
XLA Modules:
  0.0 2295.2 jit_solution(9087283934844463912)
XLA Ops:
  7.2 2.1 collective-permute-start
  9.2 0.7 reduce
  9.9 0.9 reduce-window.6
  11.2 0.7 fusion.20
  11.9 2.8 scatter_custom_fusion.1
  14.7 1.0 reshape.48
  15.6 15.7 all-to-all-start.1
  32.7 0.4 fusion.11
  33.6 2.6 collective-permute-start.1
  37.1 17.6 collective-permute-done.1
  54.6 1.9 collective-permute-start.2
  56.6 0.4 fusion.13
  57.4 17.6 collective-permute-done.2
  75.4 0.6 copy-done.3
  76.1 1.4 add_convert_fusion
  77.5 3.1 scatter_custom_fusion
  80.7 72.5 %all_to_all.10 = bf16[8,60,1024]{2,1,0:T(8,128)(2,1)S(1)} all-to-all(bf16[8,60,1024]{2,1,0:T(8,128)(2,1)S(1)} %reshape.47), channel_id=1, replica_groups=mesh['dp'=128,'expert'=8] {'expert'}, dimensions={0} | all-to-all | bytes 1966080 | tf_op jit(solution)/shard_map/all_to_all | solution.py:104
  153.2 2.6 convolution_bitcast_fusion
  155.8 0.9 copy-done.2
  157.0 2.1 collective-permute-start.3
  159.0 26.8 %collective-permute-done.3 = f32[64,1024]{1,0:T(8,128)S(1)} collective-permute-done((f32[64,1024]{1,0:T(8,128)S(1)}, f32[64,1024]{1,0:T(8,128)S(1)}, u32[]{:S(2)}, u32[]{:S(2)}) %collective-permute-start.3) | collective-permute-done | bytes 262176 | tf_op jit(solution)/shard_map/ppermute | solution.py:12
  186.1 1.9 collective-permute-start.4
  188.3 18.6 collective-permute-done.4
  206.9 1.9 collective-permute-start.5
  209.1 18.5 collective-permute-done.5
  227.7 1.9 collective-permute-start.6
  229.6 1.3 dynamic-slice
  231.6 0.6 add_add_fusion
  232.2 6.2 collective-permute-done.6
  238.3 2048.0 %all-reduce.3.cloned.1.call-done = f32[1024,640]{1,0:T(8,128)} async-done(((f32[1024,640]{1,0:T(8,128)}), f32[1024,640]{1,0:T(8,128)}) %all-reduce.3.cloned.1.call-update) | async-done | bytes 2621456
  2286.3 1.3 dynamic-slice_bitcast_fusion
  2287.7 0.7 copy.13
  (39 shorter events, 3.8 us)
Async XLA Ops:
  7.2 25.5 %copy-start = (bf16[384,1024]{1,0:T(8,128)(2,1)S(1)}, bf16[384,1024]{1,0:T(8,128)(2,1)}, u32[]{:S(2)}) copy-start(bf16[384,1024]{1,0:T(8,128)(2,1)} %param.6) | copy-start | bytes 2359300
  7.2 26.4 %collective-permute-start = (bf16[64,1024]{1,0:T(8,128)(2,1)}, bf16[64,1024]{1,0:T(8,128)(2,1)S(1)}, u32[]{:S(2)}, u32[]{:S(2)}) collective-permute-start(bf16[64,1024]{1,0:T(8,128)(2,1)} %param.7), channel_id=1, source_target_pairs={{0,8},{8,16},{16,24},{24,32},{32,40},{40,48},{48,56},{56,64},{64,7... | collective-permute-start | bytes 393224 | tf_op jit(solution)/shard_map/ppermute | solution.py:12
  11.9 20.8 copy-start.9
  15.6 65.1 %all-to-all-start.1 = ((bf16[8,60,640]{2,1,0:T(8,128)(2,1)}), bf16[8,60,640]{2,1,0:T(8,128)(2,1)S(1)}, u32[]{:S(2)}, u32[]{:S(2)}) async-start(bf16[8,60,640]{2,1,0:T(8,128)(2,1)} %reshape.48), calls=%async_computation.1 | async-start | bytes 1310720 | tf_op jit(solution)/shard_map/all_to_all | solution.py:97
  31.4 2255.0 %all-reduce.3.cloned.1.call-start = ((), (), s32[]{:S(2)}) async-start(), calls=%async_computation.2 | async-start | bytes 5242880
  33.1 3.9 copy-start.1
  33.6 21.1 collective-permute-start.1
  36.6 20.8 copy-start.5
  54.6 20.4 collective-permute-start.2
  57.0 18.0 copy-start.7
  75.4 0.6 copy-start.3
  155.8 0.9 copy-start.2
  155.8 30.0 %copy-start.6 = (f32[384,64]{0,1:T(8,128)S(1)}, f32[384,64]{0,1:T(8,128)}, u32[]{:S(2)}) copy-start(f32[384,64]{0,1:T(8,128)} %copy-done.5) | copy-start | bytes 294916
  156.7 31.3 %copy-start.8 = (f32[384,64]{0,1:T(8,128)S(1)}, f32[384,64]{0,1:T(8,128)}, u32[]{:S(2)}) copy-start(f32[384,64]{0,1:T(8,128)} %copy-done.7) | copy-start | bytes 294916
  157.0 51.9 %copy-start.4 = (f32[384,64]{0,1:T(8,128)S(1)}, f32[384,64]{0,1:T(8,128)}, u32[]{:S(2)}) copy-start(f32[384,64]{0,1:T(8,128)} %copy-done.3) | copy-start | bytes 294916
  157.0 28.9 %collective-permute-start.3 = (f32[64,1024]{1,0:T(8,128)S(1)}, f32[64,1024]{1,0:T(8,128)S(1)}, u32[]{:S(2)}, u32[]{:S(2)}) collective-permute-start(f32[64,1024]{1,0:T(8,128)S(1)} %fusion.27), channel_id=1, source_target_pairs={{0,8},{8,16},{16,24},{24,32},{32,40},{40,48},{48,56},{56,64},{64,7... | collective-permute-start | bytes 786440 | tf_op jit(solution)/shard_map/ppermute | solution.py:12
  186.1 20.8 collective-permute-start.4
  206.9 20.7 collective-permute-start.5
  227.7 10.6 collective-permute-start.6
Sparse Core Ops, SparseCore 0:
  156.0 2130.3 all-reduce.2
where the time goes:
time: 2300 us
  waiting for transfers between devices  2150 us (93%)
  blocking collectives  72.5 us (3%)
  starting transfers between devices  30.2 us (1%)
    unnamed x2, waiting for transfers between devices  2050 us
    ppermute x7, waiting for transfers between devices, from_behind(): return lax.ppermute(value, axis, pairs)  105 us
    all_to_all x1, blocking collectives, on_device(): lax.all_to_all(grad_buffer.reshape(owners, capacity, grad_width), 'expert...  72.5 us
  transfers between devices with their start and end apart: 9, of which 7 were waited for; matrix products, arithmetic and copies ran while one was open for 1% of the time, Pallas kernels for 0%

commit v1 on v0

v1 whole, which is shorter than its diff:
```python
import jax
import jax.numpy as jnp
from jax import lax
from jax.experimental import pallas as pl
from jax.experimental.pallas import tpu as pltpu
from jax.sharding import PartitionSpec as P

MESH = pl.DeviceIdType.MESH
NX, NY, NZ, ZLO = 4, 8, 16, 8
IMG, TXT, EMB, FEAT = 384, 64, 1024, 640
STEPS = 4
SLOT = 64
HALF = EMB // 2
QUART = 128
BF, F32 = jnp.bfloat16, jnp.float32


def dest_of(x, y, z, core):
    x, y, z = lax.rem(x + NX, NX), lax.rem(y + NY, NY), lax.rem(z + NZ, NZ)
    return (((z // ZLO * NX + x) * NY + y) * 2 + core, lax.rem(z, ZLO))


def offset_of(delta, core):
    sign = 1 - 2 * core
    return (
        (0, 0, 0),
        (0, 1, 0),
        (1, 0, 0),
        (0, 0, 1),
        (0, sign, sign),
        (0, 0, -1),
        (-1, 0, 0),
        (0, -1, 0),
    )[delta]


def kernel(
    img_hbm, txt_hbm, feat_hbm, ids_ref, scale_ref, shift_ref,
    loss_ref, tgrad_ref, egrad_ref,
    img, feat, txt, perm, wts, fsend, fr, ft, gsend, gr, tgs, tgr, s1s, s1r, s2s, s2r, fin_s, fin_r,
    in_sem, txt_ss, txt_rs, f_ss, f_rs, ff_ss, ff_rs, g_ss, g_rs, tg_ss, tg_rs, s1_ss, s1_rs,
    s2_ss, s2_rs, fin_ss, fin_rs,
):
    dp, ex = lax.axis_index("dp"), lax.axis_index("expert")
    n_dp = 2 * NX * NY * (NZ // ZLO)
    core = lax.rem(dp, 2)
    y = lax.rem(dp // 2, NY)
    x = lax.rem(dp // (2 * NY), NX)
    zh = dp // (2 * NY * NX)
    z = zh * ZLO + ex
    other = 1 - core
    sign = 1 - 2 * core
    residue = lax.rem(2 * x + y + 3 * z, 8)
    sibling = (dp + 1 - 2 * core, ex)

    def along(steps):
        return (lax.rem(dp + steps + n_dp, n_dp), ex)

    def remote(src, dst, ss, rs, dev):
        return pltpu.make_async_remote_copy(
            src_ref=src, dst_ref=dst, send_sem=ss, recv_sem=rs, device_id=dev, device_id_type=MESH
        )

    c_img = pltpu.make_async_copy(img_hbm, img, in_sem.at[0])
    c_feat = pltpu.make_async_copy(feat_hbm, feat, in_sem.at[1])
    c_txt = pltpu.make_async_copy(txt_hbm, txt.at[pl.ds(0, TXT)], in_sem.at[2])
    c_feat.start()
    c_txt.start()
    c_img.start()

    barrier = pltpu.get_barrier_semaphore()

    def greet(dev):
        pl.semaphore_signal(barrier, inc=1, device_id=dev, device_id_type=MESH)

    for s in range(1, STEPS):
        greet(along(-s))
        greet(along(s))
    greet(sibling)
    for delta in range(1, 8):
        for cs in range(2):
            dx, dy, dz = offset_of(delta, cs)
            greet(dest_of(x - dx, y - dy, z - dz, cs))
    greet(dest_of(x - 1, y - 1, z + 1, core))
    greet(dest_of(x + 1, y + 1, z - 1, core))
    greet(dest_of(x - 2 * sign, y - 2 * sign, z + 2 * sign, core))

    def source_y(zs):
        return lax.rem(ex + 64 - 2 * x - 3 * zs, 8)

    @pl.when(core == zh)
    def _():
        for zs in range(NZ):
            ys = source_y(zs)

            @pl.when(jnp.logical_or(ys != y, zs != z))
            def _():
                greet(dest_of(x, ys, zs, core))

    to_self = jnp.logical_and(core == zh, residue == ex)
    pl.semaphore_wait(barrier, 6 + 1 + 14 + 3 + 8 - to_self.astype(jnp.int32))

    def txt_copy(s):
        return remote(txt_hbm, txt.at[pl.ds(s * TXT, TXT)], txt_ss.at[s - 1], txt_rs.at[s - 1], along(s))

    for s in range(1, STEPS):
        txt_copy(s).start()

    rel = lax.rem(ids_ref[...] + 8 - residue, 8)
    hot = (rel == lax.broadcasted_iota(jnp.int32, (8, IMG), 0)).astype(BF)
    before = (
        lax.broadcasted_iota(jnp.int32, (IMG, IMG), 0) < lax.broadcasted_iota(jnp.int32, (IMG, IMG), 1)
    ).astype(BF)
    counts = jnp.dot(hot, before, preferred_element_type=F32)
    rank = jnp.sum(counts * hot.astype(F32), axis=0, keepdims=True)
    place = rel * SLOT + rank.astype(jnp.int32)
    perm[...] = jnp.where(
        lax.broadcasted_iota(jnp.int32, (8 * SLOT, IMG), 0) == place, 1.0, 0.0
    ).astype(BF)
    c_feat.wait()
    fsend[...] = jnp.dot(perm[...], feat[...], preferred_element_type=F32).astype(BF)

    def f_copy(delta):
        dx, dy, dz = offset_of(delta, core)
        row = pl.multiple_of((core * 8 + delta) * SLOT, SLOT)
        return remote(
            fsend.at[pl.ds(delta * SLOT, SLOT)], fr.at[pl.ds(row, SLOT)],
            f_ss.at[delta], f_rs.at[delta], dest_of(x + dx, y + dy, z + dz, core),
        )

    for delta in (4, 3, 5, 2, 6, 1, 7):
        f_copy(delta).start()
    own0 = pl.multiple_of(core * 8 * SLOT, SLOT)
    fr[pl.ds(own0, SLOT), :] = fsend[0:SLOT, :]

    scale, shift = scale_ref[0], shift_ref[0]
    c_img.wait()
    c_txt.wait()

    def pairs(first, rows, match):
        block = txt[pl.ds(first, rows), :]
        logits = scale * lax.dot_general(
            block, img[...], (((1,), (1,)), ((), ())), preferred_element_type=F32
        ) + shift
        if match:
            hit = lax.broadcasted_iota(jnp.int32, (rows, IMG), 0) == (
                lax.broadcasted_iota(jnp.int32, (rows, IMG), 1) // 2
            )
            labels = jnp.where(hit, 1.0, -1.0)
            arg = -labels * logits
            amount = -scale * labels
        else:
            arg = logits
            amount = scale
        small = jnp.exp(-jnp.abs(arg))
        loss = jnp.maximum(arg, 0.0) + jnp.log1p(small)
        inv = 1.0 / (1.0 + small)
        sig = jnp.where(arg >= 0.0, inv, small * inv)
        wts[pl.ds(first, rows), :] = (amount * sig).astype(BF)
        return jnp.sum(loss, axis=0, keepdims=True)

    loss = pairs(0, TXT, True)

    for delta in (1, 7, 2, 6, 3, 5, 4):
        f_copy(delta).wait_recv()
    half_rows = pl.ds(own0, 8 * SLOT)
    ff = remote(fr.at[half_rows], fr.at[half_rows], ff_ss, ff_rs, sibling)
    ff.start()

    for s in range(1, STEPS):
        txt_copy(s).wait_recv()
    loss_ref[...] = loss + pairs(TXT, (STEPS - 1) * TXT, False)

    picked = lax.dot_general(
        perm[...], wts[...], (((1,), (1,)), ((), ())), preferred_element_type=F32
    ).astype(BF)
    gsend[...] = jnp.dot(picked, txt[...], preferred_element_type=F32).astype(BF)

    def g_copy(delta, half):
        dx, dy, dz = offset_of(delta, core)
        row = pl.multiple_of((core * 8 + delta) * SLOT, SLOT)
        dev = sibling if delta == 0 else dest_of(x + dx, y + dy, z + dz, half)
        col = half * HALF
        if delta == 0:
            col = pl.multiple_of(other * HALF, HALF)
        return remote(
            gsend.at[pl.ds(delta * SLOT, SLOT), pl.ds(col, HALF)], gr.at[pl.ds(row, SLOT)],
            g_ss.at[delta, half], g_rs.at[core, delta], dev,
        )

    g_list = [(delta, half) for delta in (4, 3, 5, 2, 6, 1, 7) for half in range(2)] + [(0, 0)]
    for delta, half in g_list:
        g_copy(delta, half).start()
    gr[pl.ds(own0, SLOT), :] = gsend[0:SLOT, pl.ds(pl.multiple_of(core * HALF, HALF), HALF)]

    sums = jnp.dot(wts[TXT:, :], img[...], preferred_element_type=F32)
    tgs[...] = sums.astype(BF)

    def tg_copy(s):
        rows = pl.ds((s - 1) * TXT, TXT)
        return remote(tgs.at[rows], tgr.at[rows], tg_ss.at[s - 1], tg_rs.at[s - 1], along(-s))

    for s in range(1, STEPS):
        tg_copy(s).start()
    tgrad_ref[...] = jnp.dot(wts[0:TXT, :], img[...], preferred_element_type=F32)

    ff_in = remote(
        fr.at[pl.ds(pl.multiple_of(other * 8 * SLOT, SLOT), 8 * SLOT)],
        fr.at[pl.ds(pl.multiple_of(other * 8 * SLOT, SLOT), 8 * SLOT)],
        ff_ss, ff_rs, sibling,
    )
    ff_in.wait_recv()
    ft[...] = jnp.transpose(fr[...])

    def g_arrival(cs, delta):
        rows = pl.ds((cs * 8 + delta) * SLOT, SLOT)
        return remote(gr.at[rows], gr.at[rows], g_ss.at[0, 1], g_rs.at[cs, delta], sibling)

    for delta in (1, 7, 2, 6, 3, 5, 4):
        for cs in range(2):
            g_arrival(cs, delta).wait_recv()
    remote(gr.at[pl.ds(0, SLOT)], gr.at[pl.ds(0, SLOT)], g_ss.at[0, 1], g_rs.at[other, 0], sibling).wait_recv()

    def quarter(q):
        col = pl.multiple_of(lax.rem(q + NX, NX) * QUART, QUART)
        return jnp.dot(ft[...], gr[:, pl.ds(col, QUART)], preferred_element_type=F32)

    def s1_copy(i):
        step = (2 * sign, 1, -1)[i]
        return remote(
            s1s.at[i], s1r.at[i], s1_ss.at[i], s1_rs.at[i], dest_of(x + step, y + step, z - step, core)
        )

    for i, q in enumerate((x + 2, x + 1, x - 1)):
        s1s[i] = quarter(q).astype(BF)
        s1_copy(i).start()
    mine = quarter(x)
    for i in (1, 2, 0):
        s1_copy(i).wait_recv()
        mine = mine + s1r[i].astype(F32)
    s2s[...] = jnp.transpose(mine).astype(BF)

    target_z = residue + 8 * core

    def s2_copy(yt):
        row = pl.multiple_of(z * 16, 16)
        return remote(
            s2s.at[pl.ds(yt * 16, 16)], s2r.at[pl.ds(row, 16)], s2_ss.at[yt], s2_rs.at[z],
            dest_of(x, yt, target_z, core),
        )

    for yt in range(NY):
        here = jnp.logical_and(to_self, y == yt)

        @pl.when(jnp.logical_not(here))
        def _():
            s2_copy(yt).start()

        @pl.when(here)
        def _():
            s2r[pl.ds(pl.multiple_of(z * 16, 16), 16), :] = s2s[yt * 16 : yt * 16 + 16, :]

    for s in range(1, STEPS):
        tg_copy(s).wait_recv()
    tgrad_ref[...] += (
        tgr[0:TXT, :].astype(F32) + tgr[TXT : 2 * TXT, :].astype(F32) + tgr[2 * TXT :, :].astype(F32)
    )

    fin = remote(
        fin_s.at[pl.ds(pl.multiple_of(other * 8, 8), 8)], fin_r, fin_ss, fin_rs, sibling
    )

    @pl.when(core == zh)
    def _():
        for zs in range(NZ):

            @pl.when(jnp.logical_or(source_y(zs) != y, zs != z))
            def _():
                rows = pl.ds(zs * 16, 16)
                remote(s2r.at[rows], s2r.at[rows], s2_ss.at[0], s2_rs.at[zs], sibling).wait_recv()

        total = s2r[0:16, :].astype(F32)
        for zs in range(1, NZ):
            total = total + s2r[zs * 16 : zs * 16 + 16, :].astype(F32)
        fin_s[...] = total
        fin.start()
        egrad_ref[0] = fin_s[pl.ds(pl.multiple_of(core * 8, 8), 8), :]
        fin.wait_send()

    @pl.when(core != zh)
    def _():
        fin.wait_recv()
        egrad_ref[0] = fin_r[...]

    for s in range(1, STEPS):
        txt_copy(s).wait_send()
        tg_copy(s).wait_send()
    for delta in range(1, 8):
        f_copy(delta).wait_send()
    ff.wait_send()
    for delta, half in g_list:
        g_copy(delta, half).wait_send()
    for i in range(3):
        s1_copy(i).wait_send()
    for yt in range(NY):

        @pl.when(jnp.logical_not(jnp.logical_and(to_self, y == yt)))
        def _():
            s2_copy(yt).wait_send()


def on_device(images, texts, feats, ids, scale, shift):
    vmem, smem, dma = pltpu.VMEM, pltpu.SMEM, pltpu.SemaphoreType.DMA
    loss, tgrad, egrad = pl.pallas_call(
        kernel,
        out_shape=(
            jax.ShapeDtypeStruct((1, IMG), F32),
            jax.ShapeDtypeStruct((TXT, EMB), F32),
            jax.ShapeDtypeStruct((1, 8, FEAT), F32),
        ),
        in_specs=[
            pl.BlockSpec(memory_space=pl.ANY),
            pl.BlockSpec(memory_space=pl.ANY),
            pl.BlockSpec(memory_space=pl.ANY),
            pl.BlockSpec(memory_space=vmem),
            pl.BlockSpec(memory_space=smem),
            pl.BlockSpec(memory_space=smem),
        ],
        out_specs=(
            pl.BlockSpec(memory_space=vmem),
            pl.BlockSpec(memory_space=vmem),
            pl.BlockSpec(memory_space=vmem),
        ),
        scratch_shapes=[
            vmem((IMG, EMB), BF),
            vmem((IMG, FEAT), BF),
            vmem((STEPS * TXT, EMB), BF),
            vmem((8 * SLOT, IMG), BF),
            vmem((STEPS * TXT, IMG), BF),
            vmem((8 * SLOT, FEAT), BF),
            vmem((16 * SLOT, FEAT), BF),
            vmem((FEAT, 16 * SLOT), BF),
            vmem((8 * SLOT, EMB), BF),
            vmem((16 * SLOT, HALF), BF),
            vmem(((STEPS - 1) * TXT, EMB), BF),
            vmem(((STEPS - 1) * TXT, EMB), BF),
            vmem((3, FEAT, QUART), BF),
            vmem((3, FEAT, QUART), BF),
            vmem((QUART, FEAT), BF),
            vmem((NZ * 16, FEAT), BF),
            vmem((16, FEAT), F32),
            vmem((8, FEAT), F32),
            dma((3,)),
            dma((STEPS - 1,)),
            dma((STEPS - 1,)),
            dma((8,)),
            dma((8,)),
            dma,
            dma,
            dma((8, 2)),
            dma((2, 8)),
            dma((STEPS - 1,)),
            dma((STEPS - 1,)),
            dma((3,)),
            dma((3,)),
            dma((NY,)),
            dma((NZ,)),
            dma,
            dma,
        ],
        compiler_params=pltpu.CompilerParams(
            collective_id=0, has_side_effects=True, vmem_limit_bytes=48 * 1024 * 1024
        ),
        cost_estimate=pl.CostEstimate(flops=2_000_000_000, bytes_accessed=8_000_000, transcendentals=300_000),
    )(images, texts, feats, ids.reshape(1, IMG), scale, shift)
    return loss.reshape(IMG), tgrad, egrad


def solution(mesh):
    both = P(("dp", "expert"), None)
    return jax.shard_map(
        on_device,
        mesh=mesh,
        in_specs=(both, both, both, both, P(), P()),
        out_specs=(P(("dp", "expert")), both, P("expert", "dp", None)),
        check_vma=False,
    )
```

time: 2300 us -> 111 us (0.05)
  the two profiles are of different devices: /device:TPU:64 before, /device:TPU:63 now
where the time goes in v1:
time: 111 us
  Pallas kernels  104 us (94%)
  local copies, waits for them, and re-layouts  4.38 us (4%)
  between operations  1.96 us (2%)
    pallas_call x1, Pallas kernels, on_device(): pl.pallas_call(kernel, out_shape=(jax.ShapeDtypeStruct((1, IMG), F32), ja...  104 us
    unnamed x10, local copies, waits for them, and re-layouts  4.38 us

profile of v1, /device:TPU:63, one launch (start us, length us, event | category | flops | bytes accessed | tf_op | source)
XLA Modules:
  0.0 111.0 jit_solution(7577867640328090596)
XLA Ops:
  1.3 0.0 copy-start.3
  1.9 0.0 copy-done.3
  2.0 0.0 copy-start
  2.0 1.1 %copy-done = bf16[384,1024]{1,0:T(8,128)(2,1)S(1)} copy-done((bf16[384,1024]{1,0:T(8,128)(2,1)S(1)}, bf16[384,1024]{1,0:T(8,128)(2,1)}, u32[]{:S(2)}) %copy-start) | copy-done | bytes 786456
  3.1 0.0 copy-start.1
  3.1 1.0 copy-done.1
  4.1 0.0 copy-start.2
  4.1 0.9 copy-done.2
  5.0 104.1 %shard_map.85 = (f32[1,384]{1,0:T(1,128)S(1)}, f32[64,1024]{1,0:T(8,128)S(1)}, f32[1,8,640]{2,1,0:T(8,128)S(1)}) custom-call(bf16[384,1024]{1,0:T(8,128)(2,1)S(1)} %copy-done, bf16[64,1024]{1,0:T(8,128)(2,1)S(1)} %copy-done.2, bf16[384,640]{1,0:T(8,128)(2,1)S(1)} %copy-done.1, s32[1,384]{1,0:T(1,128)S(1)} %bitcast.1, f32[1]{0:T(128)S(6)} %copy.11.scale_ref, ...), custom_call_target="tpu_custom_call" | custom-call | flops 2000000000 | bytes 8000000 | tf_op jit(solution)/shard_map/pallas_call | solution.py:314
  109.1 0.6 reduce
  109.7 0.7 copy.13
  110.4 0.6 copy.14
Async XLA Ops:
  1.3 0.7 copy-start.3
  2.0 1.1 %copy-start = (bf16[384,1024]{1,0:T(8,128)(2,1)S(1)}, bf16[384,1024]{1,0:T(8,128)(2,1)}, u32[]{:S(2)}) copy-start(bf16[384,1024]{1,0:T(8,128)(2,1)} %img_hbm.1) | copy-start | bytes 2359300
  3.1 1.0 copy-start.1
  4.1 0.9 copy-start.2

commit v2 on v1

--- a/solution.py
+++ b/solution.py
@@ -10,6 +10,8 @@
 IMG, TXT, EMB, FEAT = 384, 64, 1024, 640
 STEPS = 4
 SLOT = 64
+RUN = 64
+PIECE = 128
 HALF = EMB // 2
 QUART = 128
 BF, F32 = jnp.bfloat16, jnp.float32
@@ -38,8 +40,10 @@
     img_hbm, txt_hbm, feat_hbm, ids_ref, scale_ref, shift_ref,
     loss_ref, tgrad_ref, egrad_ref,
     img, feat, txt, perm, wts, fsend, fr, ft, gsend, gr, tgs, tgr, s1s, s1r, s2s, s2r, fin_s, fin_r,
+    hop_a, hop_b, back_a, back_b,
     in_sem, txt_ss, txt_rs, f_ss, f_rs, ff_ss, ff_rs, g_ss, g_rs, tg_ss, tg_rs, s1_ss, s1_rs,
     s2_ss, s2_rs, fin_ss, fin_rs,
+    rel_ss, hop_as, hop_ar, hop_bs, hop_br, hop_cs, back_ar, back_bs, back_br, back_cs,
 ):
     dp, ex = lax.axis_index("dp"), lax.axis_index("expert")
     n_dp = 2 * NX * NY * (NZ // ZLO)
@@ -73,9 +77,18 @@
     def greet(dev):
         pl.semaphore_signal(barrier, inc=1, device_id=dev, device_id_type=MESH)
 
+    at = lax.rem(dp, RUN)
+
+    def inside(steps):
+        return jnp.logical_and(at + steps >= 0, at + steps < RUN)
+
     for s in range(1, STEPS):
-        greet(along(-s))
-        greet(along(s))
+        for steps in (-s, s):
+
+            @pl.when(inside(steps))
+            def _():
+                greet(along(steps))
+
     greet(sibling)
     for delta in range(1, 8):
         for cs in range(2):
@@ -97,14 +110,113 @@
             def _():
                 greet(dest_of(x, ys, zs, core))
 
+    lean = 2 * core - 1
+    is_relay = jnp.logical_and(jnp.logical_or(x == 1, x == 2), jnp.logical_or(y >= NY - 2, y <= 1))
+    piece = lax.rem((x - 1) * 4 + lax.rem(y + 2, NY) + 8, 8)
+    piece_cols = pl.ds(pl.multiple_of(piece * PIECE, PIECE), PIECE)
+    is_last = [at == RUN - 1 - i for i in range(3)]
+    is_first = [at == i for i in range(3)]
+
+    def relay_of(j, plane, c):
+        return dest_of(1 + j // 4, (6 + j % 4) % NY, plane, c)
+
+    def last_dev(i, plane):
+        return dest_of(NX - 1, NY - 1 - (i + 0) // 2, plane, 1 - i % 2)
+
+    def first_dev(i, plane):
+        return dest_of(0, i // 2, plane, i % 2)
+
+    @pl.when(is_relay)
+    def _():
+        greet(dest_of(x, y, z - ZLO + lean, core))
+
+        @pl.when(core == 1)
+        def _():
+            greet(last_dev(0, z - lean))
+            for i in range(3):
+                greet(first_dev(i, z - lean))
+
+        @pl.when(core == 0)
+        def _():
+            for i in (1, 2):
+                greet(last_dev(i, z - lean))
+            for i in range(2):
+                greet(first_dev(i, z - lean))
+
+    for i in range(3):
+
+        @pl.when(is_last[i])
+        def _():
+            for j in range(8):
+                greet(relay_of(j, z, 1 if i == 0 else 0))
+
+        @pl.when(is_first[i])
+        def _():
+            for j in range(8):
+                greet(relay_of(j, z, 1))
+                if i < 2:
+                    greet(relay_of(j, z, 0))
+
+    def one(flag):
+        return flag.astype(jnp.int32)
+
     to_self = jnp.logical_and(core == zh, residue == ex)
-    pl.semaphore_wait(barrier, 6 + 1 + 14 + 3 + 8 - to_self.astype(jnp.int32))
+    outs = 1 + 14 + 3 + 8 - one(to_self) + 5 * one(is_relay)
+    for s in range(1, STEPS):
+        outs = outs + one(inside(s)) + one(inside(-s))
+    for i in range(3):
+        outs = outs + 8 * one(is_last[i]) + (16 if i < 2 else 8) * one(is_first[i])
+    pl.semaphore_wait(barrier, outs)
 
     def txt_copy(s):
         return remote(txt_hbm, txt.at[pl.ds(s * TXT, TXT)], txt_ss.at[s - 1], txt_rs.at[s - 1], along(s))
 
-    for s in range(1, STEPS):
-        txt_copy(s).start()
+    def rel_copy(i, j):
+        c = 1 if i == 0 else 0
+        return remote(
+            txt_hbm.at[:, pl.ds(j * PIECE, PIECE)], hop_a.at[1 if i == 2 else 0],
+            rel_ss, hop_ar.at[1 if i == 2 else 0], relay_of(j, z + 2 * c - 1, c),
+        )
+
+    for i in range(3):
+
+        @pl.when(is_last[i])
+        def _():
+            for j in range(8):
+                rel_copy(i, j).start()
+
+    for s in (3, 2, 1):
+
+        @pl.when(inside(s))
+        def _():
+            txt_copy(s).start()
+
+    def hop_copy(slot):
+        return remote(
+            hop_a.at[slot], hop_b.at[slot], hop_as.at[slot], hop_br.at[slot],
+            dest_of(x, y, z + ZLO - lean, core),
+        )
+
+    def hop_arrival(slot):
+        return remote(hop_a.at[slot], hop_a.at[slot], hop_as.at[slot], hop_ar.at[slot], sibling)
+
+    @pl.when(is_relay)
+    def _():
+        hop_arrival(0).wait_recv()
+        hop_copy(0).start()
+
+        @pl.when(core == 0)
+        def _():
+            hop_arrival(1).wait_recv()
+            hop_copy(1).start()
+
+    fan1 = ((0, 0, 1), (0, 1, 2), (0, 2, 3))
+    fan0 = ((0, 0, 2), (0, 1, 3), (1, 0, 3))
+
+    def fan_copy(n, slot, i, s):
+        return remote(
+            hop_b.at[slot], txt.at[pl.ds(s * TXT, TXT), piece_cols], hop_cs.at[n], txt_rs.at[s - 1], first_dev(i, z)
+        )
 
     rel = lax.rem(ids_ref[...] + 8 - residue, 8)
     hot = (rel == lax.broadcasted_iota(jnp.int32, (8, IMG), 0)).astype(BF)
@@ -130,6 +242,18 @@
 
     for delta in (4, 3, 5, 2, 6, 1, 7):
         f_copy(delta).start()
+    @pl.when(is_relay)
+    def _():
+        for c, fan in ((1, fan1), (0, fan0)):
+
+            @pl.when(core == c)
+            def _():
+                for slot in range(2 - c):
+                    hop_copy(slot).wait_recv()
+                    for n in range(3):
+                        if fan[n][0] == slot:
+                            fan_copy(n, *fan[n]).start()
+
     own0 = pl.multiple_of(core * 8 * SLOT, SLOT)
     fr[pl.ds(own0, SLOT), :] = fsend[0:SLOT, :]
 
@@ -200,8 +324,27 @@
         rows = pl.ds((s - 1) * TXT, TXT)
         return remote(tgs.at[rows], tgr.at[rows], tg_ss.at[s - 1], tg_rs.at[s - 1], along(-s))
 
+    back = ((0, 1, 0, 1), (0, 2, 0, 0), (0, 3, 2, 0), (1, 2, 1, 1), (1, 3, 1, 0), (2, 3, 2, 1))
+
+    def back_out(s, slot, c, j):
+        return remote(
+            tgs.at[pl.ds((s - 1) * TXT, TXT), pl.ds(j * PIECE, PIECE)], back_a.at[slot],
+            tg_ss.at[s - 1], back_ar.at[slot], relay_of(j, z + 2 * c - 1, c),
+        )
+
+    for i, s, slot, c in back:
+
+        @pl.when(is_first[i])
+        def _():
+            for j in range(8):
+                back_out(s, slot, c, j).start()
+
     for s in range(1, STEPS):
-        tg_copy(s).start()
+
+        @pl.when(inside(-s))
+        def _():
+            tg_copy(s).start()
+
     tgrad_ref[...] = jnp.dot(wts[0:TXT, :], img[...], preferred_element_type=F32)
 
     ff_in = remote(
@@ -234,6 +377,14 @@
     for i, q in enumerate((x + 2, x + 1, x - 1)):
         s1s[i] = quarter(q).astype(BF)
         s1_copy(i).start()
+    back_copy = remote(back_a, back_b, back_bs, back_br, dest_of(x, y, z + ZLO - lean, core))
+
+    @pl.when(is_relay)
+    def _():
+        for slot in range(3):
+            remote(back_a.at[slot], back_a.at[slot], back_bs, back_ar.at[slot], sibling).wait_recv()
+        back_copy.start()
+
     mine = quarter(x)
     for i in (1, 2, 0):
         s1_copy(i).wait_recv()
@@ -259,6 +410,25 @@
         @pl.when(here)
         def _():
             s2r[pl.ds(pl.multiple_of(z * 16, 16), 16), :] = s2s[yt * 16 : yt * 16 + 16, :]
+
+    home1 = ((0, 0, 1), (1, 0, 2), (2, 0, 3))
+    home0 = ((0, 1, 2), (1, 1, 3), (2, 2, 3))
+
+    def home_copy(slot, i, s):
+        return remote(
+            back_b.at[slot], tgr.at[pl.ds((s - 1) * TXT, TXT), piece_cols],
+            back_cs.at[slot], tg_rs.at[s - 1], last_dev(i, z),
+        )
+
+    @pl.when(is_relay)
+    def _():
+        back_copy.wait_recv()
+        for c, home in ((1, home1), (0, home0)):
+
+            @pl.when(core == c)
+            def _():
+                for args in home:
+                    home_copy(*args).start()
 
     for s in range(1, STEPS):
         tg_copy(s).wait_recv()
@@ -293,8 +463,30 @@
         egrad_ref[0] = fin_r[...]
 
     for s in range(1, STEPS):
-        txt_copy(s).wait_send()
+
+        @pl.when(inside(s))
+        def _():
+            txt_copy(s).wait_send()
+
         tg_copy(s).wait_send()
+
+    @pl.when(at >= RUN - 3)
+    def _():
+        remote(txt_hbm, txt.at[pl.ds(0, TXT)], rel_ss, txt_rs.at[0], sibling).wait_send()
+
+    @pl.when(is_relay)
+    def _():
+        hop_copy(0).wait_send()
+
+        @pl.when(core == 0)
+        def _():
+            hop_copy(1).wait_send()
+
+        for n in range(3):
+            fan_copy(n, *fan1[0]).wait_send()
+            home_copy(*home1[n]).wait_send()
+        back_copy.wait_send()
+
     for delta in range(1, 8):
         f_copy(delta).wait_send()
     ff.wait_send()
@@ -350,6 +542,10 @@
             vmem((NZ * 16, FEAT), BF),
             vmem((16, FEAT), F32),
             vmem((8, FEAT), F32),
+            vmem((2, TXT, PIECE), BF),
+            vmem((2, TXT, PIECE), BF),
+            vmem((3, TXT, PIECE), BF),
+            vmem((3, TXT, PIECE), BF),
             dma((3,)),
             dma((STEPS - 1,)),
             dma((STEPS - 1,)),
@@ -367,6 +563,16 @@
             dma((NZ,)),
             dma,
             dma,
+            dma,
+            dma((2,)),
+            dma((2,)),
+            dma((2,)),
+            dma((2,)),
+            dma((3,)),
+            dma((3,)),
+            dma,
+            dma,
+            dma((3,)),
         ],
         compiler_params=pltpu.CompilerParams(
             collective_id=0, has_side_effects=True, vmem_limit_bytes=48 * 1024 * 1024

time: 111 us -> 83.7 us (0.75)
  the two profiles are of different devices: /device:TPU:63 before, /device:TPU:61 now
where the time goes in v2:
time: 83.7 us; the launch traced here: 83.4 us
  Pallas kernels  76.5 us (91%)
  local copies, waits for them, and re-layouts  4.38 us (5%)
  between operations  1.96 us (2%)
    pallas_call x1, Pallas kernels, on_device(): pl.pallas_call(kernel, out_shape=(jax.ShapeDtypeStruct((1, IMG), F32), ja...  76.5 us
    unnamed x10, local copies, waits for them, and re-layouts  4.38 us

profile of v2, /device:TPU:61, one launch (start us, length us, event | category | flops | bytes accessed | tf_op | source)
XLA Modules:
  0.0 83.4 jit_solution(18110736037736135427)
XLA Ops:
  1.3 0.0 copy-start.3
  1.9 0.0 copy-done.3
  2.0 0.0 copy-start
  2.0 1.1 %copy-done = bf16[384,1024]{1,0:T(8,128)(2,1)S(1)} copy-done((bf16[384,1024]{1,0:T(8,128)(2,1)S(1)}, bf16[384,1024]{1,0:T(8,128)(2,1)}, u32[]{:S(2)}) %copy-start) | copy-done | bytes 786456
  3.1 0.0 copy-start.1
  3.1 1.0 %copy-done.1 = bf16[384,640]{1,0:T(8,128)(2,1)S(1)} copy-done((bf16[384,640]{1,0:T(8,128)(2,1)S(1)}, bf16[384,640]{1,0:T(8,128)(2,1)}, u32[]{:S(2)}) %copy-start.1) | copy-done | bytes 491544
  4.1 0.0 copy-start.2
  4.1 0.9 %copy-done.2 = bf16[64,1024]{1,0:T(8,128)(2,1)S(1)} copy-done((bf16[64,1024]{1,0:T(8,128)(2,1)S(1)}, bf16[64,1024]{1,0:T(8,128)(2,1)}, u32[]{:S(2)}) %copy-start.2) | copy-done | bytes 131096
  5.0 76.5 %shard_map.85 = (f32[1,384]{1,0:T(1,128)S(1)}, f32[64,1024]{1,0:T(8,128)S(1)}, f32[1,8,640]{2,1,0:T(8,128)S(1)}) custom-call(bf16[384,1024]{1,0:T(8,128)(2,1)S(1)} %copy-done, bf16[64,1024]{1,0:T(8,128)(2,1)S(1)} %copy-done.2, bf16[384,640]{1,0:T(8,128)(2,1)S(1)} %copy-done.1, s32[1,384]{1,0:T(1,128)S(1)} %bitcast.1, f32[1]{0:T(128)S(6)} %copy.11.scale_ref, ...), custom_call_target="tpu_custom_call" | custom-call | flops 2000000000 | bytes 8000000 | tf_op jit(solution)/shard_map/pallas_call | solution.py:506
  81.5 0.6 reduce
  82.1 0.7 copy.13
  82.8 0.6 copy.14
Async XLA Ops:
  1.3 0.7 copy-start.3
  2.0 1.1 %copy-start = (bf16[384,1024]{1,0:T(8,128)(2,1)S(1)}, bf16[384,1024]{1,0:T(8,128)(2,1)}, u32[]{:S(2)}) copy-start(bf16[384,1024]{1,0:T(8,128)(2,1)} %img_hbm.1) | copy-start | bytes 2359300
  3.1 1.0 %copy-start.1 = (bf16[384,640]{1,0:T(8,128)(2,1)S(1)}, bf16[384,640]{1,0:T(8,128)(2,1)}, u32[]{:S(2)}) copy-start(bf16[384,640]{1,0:T(8,128)(2,1)} %feat_hbm.1) | copy-start | bytes 1474564
  4.1 0.9 %copy-start.2 = (bf16[64,1024]{1,0:T(8,128)(2,1)S(1)}, bf16[64,1024]{1,0:T(8,128)(2,1)}, u32[]{:S(2)}) copy-start(bf16[64,1024]{1,0:T(8,128)(2,1)} %txt_hbm.1) | copy-start | bytes 393220

commit v3 on v2

--- a/solution.py
+++ b/solution.py
@@ -12,8 +12,10 @@
 SLOT = 64
 RUN = 64
 PIECE = 128
+VLIM = (64 * 1024 - 320) * 1024
 HALF = EMB // 2
 QUART = 128
+CHUNKS = ((0, 384), (384, 640))
 BF, F32 = jnp.bfloat16, jnp.float32
 
 
@@ -43,7 +45,7 @@
     hop_a, hop_b, back_a, back_b,
     in_sem, txt_ss, txt_rs, f_ss, f_rs, ff_ss, ff_rs, g_ss, g_rs, tg_ss, tg_rs, s1_ss, s1_rs,
     s2_ss, s2_rs, fin_ss, fin_rs,
-    rel_ss, hop_as, hop_ar, hop_bs, hop_br, hop_cs, back_ar, back_bs, back_br, back_cs,
+    hand_ss, rel_ss, hop_as, hop_ar, hop_bs, hop_br, hop_cs, back_ar, back_bs, back_br, back_cs,
 ):
     dp, ex = lax.axis_index("dp"), lax.axis_index("expert")
     n_dp = 2 * NX * NY * (NZ // ZLO)
@@ -185,11 +187,18 @@
             for j in range(8):
                 rel_copy(i, j).start()
 
-    for s in (3, 2, 1):
-
-        @pl.when(inside(s))
+    sends = ((2, inside(2)), (3, jnp.logical_and(core == 1, inside(3))), (1, core == 0))
+    for s, flag in sends:
+
+        @pl.when(flag)
         def _():
             txt_copy(s).start()
+
+    hand = 3 - 2 * core
+    handed = remote(
+        txt.at[pl.ds(2 * TXT, TXT)], txt.at[pl.ds(pl.multiple_of(hand * TXT, TXT), TXT)],
+        hand_ss, txt_rs.at[hand - 1], sibling,
+    )
 
     def hop_copy(slot):
         return remote(
@@ -285,15 +294,21 @@
 
     loss = pairs(0, TXT, True)
 
+    txt_copy(2).wait_recv()
+
+    @pl.when(at >= 2)
+    def _():
+        handed.start()
+
     for delta in (1, 7, 2, 6, 3, 5, 4):
         f_copy(delta).wait_recv()
     half_rows = pl.ds(own0, 8 * SLOT)
     ff = remote(fr.at[half_rows], fr.at[half_rows], ff_ss, ff_rs, sibling)
     ff.start()
 
-    for s in range(1, STEPS):
-        txt_copy(s).wait_recv()
-    loss_ref[...] = loss + pairs(TXT, (STEPS - 1) * TXT, False)
+    txt_copy(1).wait_recv()
+    txt_copy(3).wait_recv()
+    loss_ref[...] = (loss + pairs(TXT, (STEPS - 1) * TXT, False)).reshape(IMG)
 
     picked = lax.dot_general(
         perm[...], wts[...], (((1,), (1,)), ((), ())), preferred_element_type=F32
@@ -364,19 +379,26 @@
             g_arrival(cs, delta).wait_recv()
     remote(gr.at[pl.ds(0, SLOT)], gr.at[pl.ds(0, SLOT)], g_ss.at[0, 1], g_rs.at[other, 0], sibling).wait_recv()
 
-    def quarter(q):
+    def quarter(q, k):
         col = pl.multiple_of(lax.rem(q + NX, NX) * QUART, QUART)
-        return jnp.dot(ft[...], gr[:, pl.ds(col, QUART)], preferred_element_type=F32)
-
-    def s1_copy(i):
+        lo, hi = CHUNKS[k]
+        return jnp.dot(ft[lo:hi, :], gr[:, pl.ds(col, QUART)], preferred_element_type=F32)
+
+    def s1_copy(k, i):
         step = (2 * sign, 1, -1)[i]
-        return remote(
-            s1s.at[i], s1r.at[i], s1_ss.at[i], s1_rs.at[i], dest_of(x + step, y + step, z - step, core)
-        )
-
-    for i, q in enumerate((x + 2, x + 1, x - 1)):
-        s1s[i] = quarter(q).astype(BF)
-        s1_copy(i).start()
+        lo, hi = CHUNKS[k]
+        rows = pl.ds(lo, hi - lo)
+        return remote(
+            s1s.at[i, rows], s1r.at[i, rows], s1_ss.at[k, i], s1_rs.at[k, i],
+            dest_of(x + step, y + step, z - step, core),
+        )
+
+    for k in range(2):
+        lo, hi = CHUNKS[k]
+        for i, q in enumerate((x + 2, x + 1, x - 1)):
+            s1s[i, lo:hi, :] = quarter(q, k).astype(BF)
+            s1_copy(k, i).start()
+
     back_copy = remote(back_a, back_b, back_bs, back_br, dest_of(x, y, z + ZLO - lean, core))
 
     @pl.when(is_relay)
@@ -385,31 +407,35 @@
             remote(back_a.at[slot], back_a.at[slot], back_bs, back_ar.at[slot], sibling).wait_recv()
         back_copy.start()
 
-    mine = quarter(x)
-    for i in (1, 2, 0):
-        s1_copy(i).wait_recv()
-        mine = mine + s1r[i].astype(F32)
-    s2s[...] = jnp.transpose(mine).astype(BF)
-
     target_z = residue + 8 * core
 
-    def s2_copy(yt):
+    def s2_copy(k, yt):
         row = pl.multiple_of(z * 16, 16)
-        return remote(
-            s2s.at[pl.ds(yt * 16, 16)], s2r.at[pl.ds(row, 16)], s2_ss.at[yt], s2_rs.at[z],
+        lo, hi = CHUNKS[k]
+        cols = pl.ds(lo, hi - lo)
+        return remote(
+            s2s.at[pl.ds(yt * 16, 16), cols], s2r.at[pl.ds(row, 16), cols], s2_ss.at[k, yt], s2_rs.at[k, z],
             dest_of(x, yt, target_z, core),
         )
 
-    for yt in range(NY):
-        here = jnp.logical_and(to_self, y == yt)
-
-        @pl.when(jnp.logical_not(here))
-        def _():
-            s2_copy(yt).start()
-
-        @pl.when(here)
-        def _():
-            s2r[pl.ds(pl.multiple_of(z * 16, 16), 16), :] = s2s[yt * 16 : yt * 16 + 16, :]
+    mines = [quarter(x, k) for k in range(2)]
+    for k in range(2):
+        lo, hi = CHUNKS[k]
+        mine = mines[k]
+        for i in (1, 2, 0):
+            s1_copy(k, i).wait_recv()
+            mine = mine + s1r[i, lo:hi, :].astype(F32)
+        s2s[:, lo:hi] = jnp.transpose(mine).astype(BF)
+        for yt in range(NY):
+            here = jnp.logical_and(to_self, y == yt)
+
+            @pl.when(jnp.logical_not(here))
+            def _():
+                s2_copy(k, yt).start()
+
+            @pl.when(here)
+            def _():
+                s2r[pl.ds(pl.multiple_of(z * 16, 16), 16), lo:hi] = s2s[yt * 16 : yt * 16 + 16, lo:hi]
 
     home1 = ((0, 0, 1), (1, 0, 2), (2, 0, 3))
     home0 = ((0, 1, 2), (1, 1, 3), (2, 2, 3))
@@ -436,39 +462,50 @@
         tgr[0:TXT, :].astype(F32) + tgr[TXT : 2 * TXT, :].astype(F32) + tgr[2 * TXT :, :].astype(F32)
     )
 
-    fin = remote(
-        fin_s.at[pl.ds(pl.multiple_of(other * 8, 8), 8)], fin_r, fin_ss, fin_rs, sibling
-    )
+    def fin_copy(k):
+        lo, hi = CHUNKS[k]
+        cols = pl.ds(lo, hi - lo)
+        return remote(
+            fin_s.at[pl.ds(pl.multiple_of(other * 8, 8), 8), cols], fin_r.at[:, cols], fin_ss.at[k], fin_rs.at[k], sibling
+        )
 
     @pl.when(core == zh)
     def _():
-        for zs in range(NZ):
-
-            @pl.when(jnp.logical_or(source_y(zs) != y, zs != z))
-            def _():
-                rows = pl.ds(zs * 16, 16)
-                remote(s2r.at[rows], s2r.at[rows], s2_ss.at[0], s2_rs.at[zs], sibling).wait_recv()
-
-        total = s2r[0:16, :].astype(F32)
-        for zs in range(1, NZ):
-            total = total + s2r[zs * 16 : zs * 16 + 16, :].astype(F32)
-        fin_s[...] = total
-        fin.start()
+        for k in range(2):
+            lo, hi = CHUNKS[k]
+            for zs in range(NZ):
+
+                @pl.when(jnp.logical_or(source_y(zs) != y, zs != z))
+                def _():
+                    block = s2r.at[pl.ds(zs * 16, 16), pl.ds(lo, hi - lo)]
+                    remote(block, block, s2_ss.at[k, 0], s2_rs.at[k, zs], sibling).wait_recv()
+
+            total = s2r[0:16, lo:hi].astype(F32)
+            for zs in range(1, NZ):
+                total = total + s2r[zs * 16 : zs * 16 + 16, lo:hi].astype(F32)
+            fin_s[:, lo:hi] = total
+            fin_copy(k).start()
         egrad_ref[0] = fin_s[pl.ds(pl.multiple_of(core * 8, 8), 8), :]
-        fin.wait_send()
+        for k in range(2):
+            fin_copy(k).wait_send()
 
     @pl.when(core != zh)
     def _():
-        fin.wait_recv()
+        for k in range(2):
+            fin_copy(k).wait_recv()
         egrad_ref[0] = fin_r[...]
 
-    for s in range(1, STEPS):
-
-        @pl.when(inside(s))
+    for s, flag in sends:
+
+        @pl.when(flag)
         def _():
             txt_copy(s).wait_send()
 
         tg_copy(s).wait_send()
+
+    @pl.when(at >= 2)
+    def _():
+        handed.wait_send()
 
     @pl.when(at >= RUN - 3)
     def _():
@@ -492,13 +529,14 @@
     ff.wait_send()
     for delta, half in g_list:
         g_copy(delta, half).wait_send()
-    for i in range(3):
-        s1_copy(i).wait_send()
-    for yt in range(NY):
-
-        @pl.when(jnp.logical_not(jnp.logical_and(to_self, y == yt)))
-        def _():
-            s2_copy(yt).wait_send()
+    for k in range(2):
+        for i in range(3):
+            s1_copy(k, i).wait_send()
+        for yt in range(NY):
+
+            @pl.when(jnp.logical_not(jnp.logical_and(to_self, y == yt)))
+            def _():
+                s2_copy(k, yt).wait_send()
 
 
 def on_device(images, texts, feats, ids, scale, shift):
@@ -506,7 +544,7 @@
     loss, tgrad, egrad = pl.pallas_call(
         kernel,
         out_shape=(
-            jax.ShapeDtypeStruct((1, IMG), F32),
+            jax.ShapeDtypeStruct((IMG,), F32),
             jax.ShapeDtypeStruct((TXT, EMB), F32),
             jax.ShapeDtypeStruct((1, 8, FEAT), F32),
         ),
@@ -557,11 +595,12 @@
             dma((2, 8)),
             dma((STEPS - 1,)),
             dma((STEPS - 1,)),
-            dma((3,)),
-            dma((3,)),
-            dma((NY,)),
-            dma((NZ,)),
-            dma,
+            dma((2, 3)),
+            dma((2, 3)),
+            dma((2, NY)),
+            dma((2, NZ)),
+            dma((2,)),
+            dma((2,)),
             dma,
             dma,
             dma((2,)),
@@ -575,11 +614,11 @@
             dma((3,)),
         ],
         compiler_params=pltpu.CompilerParams(
-            collective_id=0, has_side_effects=True, vmem_limit_bytes=48 * 1024 * 1024
+            collective_id=0, has_side_effects=True, vmem_limit_bytes=VLIM
         ),
         cost_estimate=pl.CostEstimate(flops=2_000_000_000, bytes_accessed=8_000_000, transcendentals=300_000),
     )(images, texts, feats, ids.reshape(1, IMG), scale, shift)
-    return loss.reshape(IMG), tgrad, egrad
+    return loss, tgrad, egrad
 
 
 def solution(mesh):

time: 83.7 us -> 80.8 us (0.965)
  the two profiles are of different devices: /device:TPU:61 before, /device:TPU:191 now
where the time goes in v3:
time: 80.8 us; the launch traced here: 80.5 us
  Pallas kernels  75.1 us (93%)
  local copies, waits for them, and re-layouts  3.54 us (4%)
  between operations  1.94 us (2%)
    pallas_call x1, Pallas kernels, on_device(): pl.pallas_call(kernel, out_shape=(jax.ShapeDtypeStruct((IMG,), F32), jax....  75.1 us
    unnamed x7, local copies, waits for them, and re-layouts  3.54 us

profile of v3, /device:TPU:191, one launch (start us, length us, event | category | flops | bytes accessed | tf_op | source)
XLA Modules:
  0.0 80.5 jit_solution(1552234766238566455)
XLA Ops:
  1.9 75.1 %shard_map.85 = (f32[384]{0:T(512)}, f32[64,1024]{1,0:T(8,128)}, f32[1,8,640]{2,1,0:T(8,128)}) custom-call(bf16[384,1024]{1,0:T(8,128)(2,1)} %img_hbm.1, bf16[64,1024]{1,0:T(8,128)(2,1)} %txt_hbm.1, bf16[384,640]{1,0:T(8,128)(2,1)} %feat_hbm.1, s32[1,384]{1,0:T(1,128)} %bitcast.1, f32[1]{0:T(128)S(6)} %copy.12.scale_ref, f32[1]{0:T(128)S(6)} %copy.13.shift_ref), custom_call_target="tpu_custom_call" | custom-call | flops 2000000000 | bytes 8000000 | tf_op jit(solution)/shard_map/pallas_call | solution.py:544
  77.0 0.0 copy-start.1
  77.0 0.7 copy-done.1
  77.7 0.6 copy.14
  78.2 0.0 copy-start
  78.3 1.7 %copy.15 = f32[64,1024]{1,0:T(8,128)} copy(f32[64,1024]{1,0:T(8,128)} %get-tuple-element.7) | data formatting | bytes 524288
  79.9 0.0 copy-done
  79.9 0.6 copy.16
Async XLA Ops:
  77.0 0.7 copy-start.1
  78.2 1.7 %copy-start = (f32[1,8,640]{2,1,0:T(8,128)S(1)}, f32[1,8,640]{2,1,0:T(8,128)}, u32[]{:S(2)}) copy-start(f32[1,8,640]{2,1,0:T(8,128)} %get-tuple-element.8) | copy-start | bytes 61444
